TPU v7x, 32 devices: a whole 2x2x4 slice. The times are simulated.
32 devices in a mesh: ctx: 16 (over z, y, core), uly: 2 (over x).
Axes of the slice: x: 2, y: 2, z: 4, core: 2. Of those that a mesh axis runs over, the one named last changes fastest.
Arguments:
- queries: bfloat16 [4096, 4096], P(('ctx', 'uly')), may hold values from -200 to 200, as said below
- keys: bfloat16 [4096, 1024], P(('ctx', 'uly')), may hold values from -6 to 6, as said below
- values: bfloat16 [4096, 1024], P(('ctx', 'uly')), may hold values from -6 to 6
Outputs:
- attended: bfloat16 [4096, 4096], P(('ctx', 'uly'))
Inputs may be any that keep to these rules, and one draw needn't show every extreme that they name: `queries`: entries of order one, except that some query rows may be large. `keys`: entries of order one.
All inputs are finite; a program needn't handle non-finite values.
Results may differ from a plain program's by a relative error of at most 0.0055.
Values may be sent and summed in bfloat16 or wider, within the bound.
A program may use at most 64 MiB of HBM per device.

v0:
```python
import jax
import jax.numpy as jnp
from jax import lax
from jax.sharding import PartitionSpec as P

HEAD_SIZE = 128
WINDOW_BLOCKS = 3


def passed_along(block, axis, distance):
    devices = range(lax.axis_size(axis))
    route = [(i - distance, i) for i in devices if i - distance in devices]
    return lax.ppermute(block, axis, route)


def on_device(queries, keys, values):
    scale_factor = HEAD_SIZE ** (-0.5)
    cycle_pos = lax.axis_index("ctx")
    query_here, key_here, value_here = (
        lax.all_to_all(queries, "uly", split_axis=1, concat_axis=0, tiled=True),
        lax.all_to_all(keys, "uly", split_axis=1, concat_axis=0, tiled=True),
        lax.all_to_all(values, "uly", split_axis=1, concat_axis=0, tiled=True),
    )
    block_len = query_here.shape[0]
    q_heads = query_here.shape[1] // HEAD_SIZE
    kv_heads = key_here.shape[1] // HEAD_SIZE
    group_size = q_heads // kv_heads
    row_block = min(block_len, 512)
    pieces = block_len // row_block
    item_count = q_heads * pieces
    query_items = (
        query_here.reshape(block_len, q_heads, HEAD_SIZE)
        .transpose(1, 0, 2)
        .reshape(item_count, row_block, HEAD_SIZE)
    )
    key_blocks = key_here.reshape(block_len, kv_heads, HEAD_SIZE).transpose(1, 0, 2)
    value_blocks = value_here.reshape(block_len, kv_heads, HEAD_SIZE).transpose(1, 0, 2)
    carry_state = (
        jnp.full((item_count, row_block), -1e30, jnp.float32),
        jnp.zeros((item_count, row_block), jnp.float32),
        jnp.zeros((item_count, row_block, HEAD_SIZE), jnp.float32),
    )

    def absorb(carry_state, key_set, value_set, step_back):

        def per_item(inputs):
            item_index, running_max, running_sum, weighted, query_rows = inputs
            key_value_index = item_index // (pieces * group_size)
            key_rows = lax.dynamic_index_in_dim(key_set, key_value_index, 0, keepdims=False)
            value_rows = lax.dynamic_index_in_dim(value_set, key_value_index, 0, keepdims=False)
            scores = (
                jnp.einsum("qd,td->qt", query_rows, key_rows, preferred_element_type=jnp.float32)
                * scale_factor
            )
            if step_back == 0:
                query_pos = item_index % pieces * row_block + jnp.arange(row_block, dtype=jnp.int32)
                key_pos = jnp.arange(block_len, dtype=jnp.int32)
                visible = key_pos[None, :] <= query_pos[:, None]
            else:
                visible = jnp.broadcast_to(cycle_pos >= step_back, scores.shape)
            scores = jnp.where(visible, scores, jnp.float32(-1e30))
            new_max = jnp.maximum(running_max, jnp.max(scores, axis=-1))
            weights = jnp.where(visible, jnp.exp(scores - new_max[:, None]), jnp.float32(0.0))
            factor = jnp.exp(running_max - new_max)
            new_sum = running_sum * factor + jnp.sum(weights, axis=-1)
            product = jnp.einsum(
                "qt,td->qd",
                weights.astype(jnp.bfloat16),
                value_rows,
                preferred_element_type=jnp.float32,
            )
            return (new_max, new_sum, weighted * factor[:, None] + product)

        return lax.map(
            per_item,
            (
                jnp.arange(item_count, dtype=jnp.int32),
                carry_state[0],
                carry_state[1],
                carry_state[2],
                query_items,
            ),
        )

    carry_state = absorb(carry_state, key_blocks, value_blocks, 0)
    current = (key_blocks, value_blocks)
    for step_back in range(1, WINDOW_BLOCKS + 1):
        current = passed_along((current[0], current[1]), "ctx", 1)
        carry_state = absorb(carry_state, current[0], current[1], step_back)
    output_rows = (carry_state[2] / carry_state[1][..., None]).astype(jnp.bfloat16)
    output_rows = (
        output_rows.reshape(q_heads, block_len, HEAD_SIZE)
        .transpose(1, 0, 2)
        .reshape(block_len, q_heads * HEAD_SIZE)
    )
    return lax.all_to_all(output_rows, "uly", split_axis=0, concat_axis=1, tiled=True)


def solution(mesh):
    placed = (P(("ctx", "uly"), None), P(("ctx", "uly"), None), P(("ctx", "uly"), None))
    return jax.shard_map(
        on_device, mesh=mesh, in_specs=placed, out_specs=P(("ctx", "uly"), None), check_vma=False
    )
```

profile of v0, /device:TPU:0, one launch (start us, length us, event | category | flops | bytes accessed | tf_op | source)
XLA Modules:
  0.0 406.8 jit_solution(9087742749585200211)
XLA Ops:
  0.0 1.8 copy.47
  1.8 4.2 %all-to-all-start.1 = ((bf16[128,2,512]{2,0,1:T(8,128)(2,1)}), bf16[128,2,512]{2,0,1:T(8,128)(2,1)S(1)}, u32[]{:S(2)}, u32[]{:S(2)}) async-start(bf16[128,2,512]{2,0,1:T(8,128)(2,1)} %bitcast.120), calls=%async_computation.1 | async-start | bytes 524288 | tf_op jit(solution)/shard_map/all_to_all | solution.py:21
  7.6 4.2 %all-to-all-done.1 = bf16[128,2,512]{2,0,1:T(8,128)(2,1)S(1)} async-done(((bf16[128,2,512]{2,0,1:T(8,128)(2,1)}), bf16[128,2,512]{2,0,1:T(8,128)(2,1)S(1)}, u32[]{:S(2)}, u32[]{:S(2)}) %all-to-all-start.1) | async-done | bytes 262176 | tf_op jit(solution)/shard_map/all_to_all | solution.py:21
  11.8 3.4 all-to-all-start.2
  16.4 4.1 %all-to-all-done.2 = bf16[128,2,512]{2,0,1:T(8,128)(2,1)S(1)} async-done(((bf16[128,2,512]{2,0,1:T(8,128)(2,1)}), bf16[128,2,512]{2,0,1:T(8,128)(2,1)S(1)}, u32[]{:S(2)}, u32[]{:S(2)}) %all-to-all-start.2) | async-done | bytes 262176 | tf_op jit(solution)/shard_map/all_to_all | solution.py:22
  20.4 3.6 all-to-all-start
  24.1 2.0 collective-permute-start
  26.2 4.4 %collective-permute-start.1 = (bf16[4,256,128]{2,0,1:T(4,128)(2,1)S(1)}, bf16[4,256,128]{2,0,1:T(4,128)(2,1)}, u32[]{:S(2)}, u32[]{:S(2)}) collective-permute-start(bf16[4,256,128]{2,0,1:T(4,128)(2,1)S(1)} %bitcast.194), channel_id=1, source_target_pairs={{0,2},{2,4},{4,6},{6,8},{8,10},{10,12},{12,14},{14,16},{16,18},{18... | collective-permute-start | bytes 786440 | tf_op jit(solution)/shard_map/ppermute | solution.py:13
  33.0 2.0 collective-permute-start.2
  36.7 4.2 %collective-permute-start.3 = (bf16[4,256,128]{2,0,1:T(4,128)(2,1)}, bf16[4,256,128]{2,0,1:T(4,128)(2,1)}, u32[]{:S(2)}, u32[]{:S(2)}) collective-permute-start(bf16[4,256,128]{2,0,1:T(4,128)(2,1)} %collective-permute-done.1), channel_id=1, source_target_pairs={{0,2},{2,4},{4,6},{6,8},{8,10},{10,12},{12,14},{14,16},{16,18},{18... | collective-permute-start | bytes 786440 | tf_op jit(solution)/shard_map/ppermute | solution.py:13
  41.7 88.9 %while.62 = (s32[]{:T(128)}, f32[16,256]{1,0:T(8,128)S(1)}, f32[16,256]{1,0:T(8,128)S(1)}, f32[16,256,128]{2,1,0:T(8,128)S(1)}, bf16[16,256,128]{2,1,0:T(8,128)(...) while((s32[]{:T(128)}, f32[16,256]{1,0:T(8,128)S(1)}, ...), condition=%wide.region_3.4_spmd, body=%wide.region_0.3_spmd.sunk | while | flops 34374676 | bytes 1130841 | solution.py:74
  132.2 86.3 %while.63 = (s32[]{:T(128)}, f32[16,256]{1,0:T(8,128)S(1)}, f32[16,256]{1,0:T(8,128)S(1)}, f32[16,256,128]{2,1,0:T(8,128)}, f32[16,256]{1,0:T(8,128)S(1)}, /*ind...) while((s32[]{:T(128)}, f32[16,256]{1,0:T(8,128)S(1)}, ...), condition=%wide.region_7.8_spmd, body=%wide.region_4.7_spmd.sunk | while | flops 34210836 | bytes 1268103 | solution.py:74
  135.7 1.7 fusion.116
  151.9 1.8 fusion.116
  173.4 1.7 fusion.116
  189.6 1.7 fusion.116
  200.4 1.7 fusion.116
  211.2 1.8 fusion.116
  216.6 1.8 fusion.116
  219.5 2.0 collective-permute-start.4
  223.3 4.4 %collective-permute-start.5 = (bf16[4,256,128]{2,0,1:T(4,128)(2,1)}, bf16[4,256,128]{2,0,1:T(4,128)(2,1)}, u32[]{:S(2)}, u32[]{:S(2)}) collective-permute-start(bf16[4,256,128]{2,0,1:T(4,128)(2,1)} %collective-permute-done.3), channel_id=1, source_target_pairs={{0,2},{2,4},{4,6},{6,8},{8,10},{10,12},{12,14},{14,16},{16,18},{18... | collective-permute-start | bytes 786440 | tf_op jit(solution)/shard_map/ppermute | solution.py:13
  227.8 80.2 %while.64 = (s32[]{:T(128)}, f32[16,256]{1,0:T(8,128)S(1)}, f32[16,256]{1,0:T(8,128)S(1)}, f32[16,256,128]{2,1,0:T(8,128)S(1)}, f32[16,256]{1,0:T(8,128)S(1)}, /...) while((s32[]{:T(128)}, f32[16,256]{1,0:T(8,128)S(1)}, ...), condition=%wide.region_11.12_spmd, body=%wide.region_8.11_spmd.sunk | while | flops 34210836 | bytes 1268103 | solution.py:74
  311.2 75.6 %while.65 = (s32[]{:T(128)}, f32[16,256]{1,0:T(8,128)S(1)}, f32[16,256,128]{2,1,0:T(8,128)S(1)}, f32[16,256]{1,0:T(8,128)S(1)}, f32[16,256]{1,0:T(8,128)S(1)}, /...) while((s32[]{:T(128)}, f32[16,256]{1,0:T(8,128)S(1)}, ...), condition=%wide.region_15.16_spmd, body=%wide.region_12.15_spmd.sunk | while | flops 34210836 | bytes 1265019 | solution.py:74
  388.7 16.2 %all_to_all.67 = bf16[2,128,2048]{2,1,0:T(8,128)(2,1)S(1)} all-to-all(bf16[2,128,2048]{2,1,0:T(8,128)(2,1)S(1)} %all_to_all.59), channel_id=1, replica_groups=mesh['ctx'=16,'uly'=2] {'uly'}, dimensions={0} | all-to-all | bytes 2097152 | tf_op jit(solution)/shard_map/all_to_all | solution.py:96
  (582 shorter events, 168.0 us)
Async XLA Ops:
  0.0 15.3 %copy-start.1 = (bf16[128,4096]{1,0:T(8,128)(2,1)S(1)}, bf16[128,4096]{1,0:T(8,128)(2,1)}, u32[]{:S(2)}) copy-start(bf16[128,4096]{1,0:T(8,128)(2,1)} %param.11) | copy-start | bytes 3145732
  1.8 10.1 %all-to-all-start.1 = ((bf16[128,2,512]{2,0,1:T(8,128)(2,1)}), bf16[128,2,512]{2,0,1:T(8,128)(2,1)S(1)}, u32[]{:S(2)}, u32[]{:S(2)}) async-start(bf16[128,2,512]{2,0,1:T(8,128)(2,1)} %bitcast.120), calls=%async_computation.1 | async-start | bytes 524288 | tf_op jit(solution)/shard_map/all_to_all | solution.py:21
  11.8 8.6 %all-to-all-start.2 = ((bf16[128,2,512]{2,0,1:T(8,128)(2,1)}), bf16[128,2,512]{2,0,1:T(8,128)(2,1)S(1)}, u32[]{:S(2)}, u32[]{:S(2)}) async-start(bf16[128,2,512]{2,0,1:T(8,128)(2,1)} %bitcast.119), calls=%async_computation.2 | async-start | bytes 524288 | tf_op jit(solution)/shard_map/all_to_all | solution.py:22
  20.4 20.5 %all-to-all-start = ((bf16[128,2,2048]{2,0,1:T(8,128)(2,1)}), bf16[128,2,2048]{2,0,1:T(8,128)(2,1)S(1)}, u32[]{:S(2)}, u32[]{:S(2)}) async-start(bf16[128,2,2048]{2,0,1:T(8,128)(2,1)} %bitcast.118), calls=%async_computation | async-start | bytes 2097152 | tf_op jit(solution)/shard_map/all_to_all | solution.py:20
  24.1 7.9 %collective-permute-start = (bf16[4,256,128]{2,0,1:T(4,128)(2,1)S(1)}, bf16[4,256,128]{2,0,1:T(4,128)(2,1)}, u32[]{:S(2)}, u32[]{:S(2)}) collective-permute-start(bf16[4,256,128]{2,0,1:T(4,128)(2,1)S(1)} %bitcast.196), channel_id=1, source_target_pairs={{0,2},{2,4},{4,6},{6,8},{8,10},{10,12},{12,14},{14,16},{16,18},{18... | collective-permute-start | bytes 786440 | tf_op jit(solution)/shard_map/ppermute | solution.py:13
  26.2 8.9 %collective-permute-start.1 = (bf16[4,256,128]{2,0,1:T(4,128)(2,1)S(1)}, bf16[4,256,128]{2,0,1:T(4,128)(2,1)}, u32[]{:S(2)}, u32[]{:S(2)}) collective-permute-start(bf16[4,256,128]{2,0,1:T(4,128)(2,1)S(1)} %bitcast.194), channel_id=1, source_target_pairs={{0,2},{2,4},{4,6},{6,8},{8,10},{10,12},{12,14},{14,16},{16,18},{18... | collective-permute-start | bytes 786440 | tf_op jit(solution)/shard_map/ppermute | solution.py:13
  33.0 185.5 %collective-permute-start.2 = (bf16[4,256,128]{2,0,1:T(4,128)(2,1)}, bf16[4,256,128]{2,0,1:T(4,128)(2,1)}, u32[]{:S(2)}, u32[]{:S(2)}) collective-permute-start(bf16[4,256,128]{2,0,1:T(4,128)(2,1)} %collective-permute-done), channel_id=1, source_target_pairs={{0,2},{2,4},{4,6},{6,8},{8,10},{10,12},{12,14},{14,16},{16,18},{18... | collective-permute-start | bytes 786440 | tf_op jit(solution)/shard_map/ppermute | solution.py:13
  36.7 184.8 %collective-permute-start.3 = (bf16[4,256,128]{2,0,1:T(4,128)(2,1)}, bf16[4,256,128]{2,0,1:T(4,128)(2,1)}, u32[]{:S(2)}, u32[]{:S(2)}) collective-permute-start(bf16[4,256,128]{2,0,1:T(4,128)(2,1)} %collective-permute-done.1), channel_id=1, source_target_pairs={{0,2},{2,4},{4,6},{6,8},{8,10},{10,12},{12,14},{14,16},{16,18},{18... | collective-permute-start | bytes 786440 | tf_op jit(solution)/shard_map/ppermute | solution.py:13
  219.5 88.5 %collective-permute-start.4 = (bf16[4,256,128]{2,0,1:T(4,128)(2,1)}, bf16[4,256,128]{2,0,1:T(4,128)(2,1)}, u32[]{:S(2)}, u32[]{:S(2)}) collective-permute-start(bf16[4,256,128]{2,0,1:T(4,128)(2,1)} %collective-permute-done.2), channel_id=1, source_target_pairs={{0,2},{2,4},{4,6},{6,8},{8,10},{10,12},{12,14},{14,16},{16,18},{18... | collective-permute-start | bytes 786440 | tf_op jit(solution)/shard_map/ppermute | solution.py:13
  223.3 86.0 %collective-permute-start.5 = (bf16[4,256,128]{2,0,1:T(4,128)(2,1)}, bf16[4,256,128]{2,0,1:T(4,128)(2,1)}, u32[]{:S(2)}, u32[]{:S(2)}) collective-permute-start(bf16[4,256,128]{2,0,1:T(4,128)(2,1)} %collective-permute-done.3), channel_id=1, source_target_pairs={{0,2},{2,4},{4,6},{6,8},{8,10},{10,12},{12,14},{14,16},{16,18},{18... | collective-permute-start | bytes 786440 | tf_op jit(solution)/shard_map/ppermute | solution.py:13
  308.0 2.9 copy-start
where the time goes:
time: 413 us; the launch traced here: 407 us
  loops' own time  170 us (41%)
  matrix products  111 us (27%)
  local copies, waits for them, and re-layouts  63.9 us (15%)
  starting transfers between devices  30.3 us (7%)
  blocking collectives  16.2 us (4%)
  waiting for transfers between devices  8.3 us (2%)
  other arithmetic  6.78 us (2%)
    another operation x4, loops' own time, absorb(): lax.map(per_item, (jnp.arange(item_count, dtype=jnp.int32), carry_state[0...  170 us
    dot_general x64, matrix products, per_item(): jnp.einsum('qt,td->qd', weights.astype(jnp.bfloat16), value_rows, preferr...  83.4 us
    dynamic_slice x112, local copies, waits for them, and re-layouts, absorb(): lax.map(per_item, (jnp.arange(item_count, dtype=jnp.int32), carry_state[0...  39 us
    dot_general x64, matrix products, per_item(): jnp.einsum('qd,td->qt', query_rows, key_rows, preferred_element_type=jnp....  27.9 us
    ppermute x6, starting transfers between devices, passed_along(): return lax.ppermute(block, axis, route)  19 us
    all_to_all x1, blocking collectives, on_device(): lax.all_to_all(output_rows, 'uly', split_axis=0, concat_axis=1, tiled=True)  16.2 us
    while x9, local copies, waits for them, and re-layouts, absorb(): lax.map(per_item, (jnp.arange(item_count, dtype=jnp.int32), carry_state[0...  9.97 us
  transfers between devices with their start and end apart: 9, of which 2 were waited for; matrix products, arithmetic and copies ran while one was open for 34% of the time, Pallas kernels for 0%

commit v1 on v0

--- a/solution.py
+++ b/solution.py
@@ -1,6 +1,10 @@
+import functools
+
 import jax
 import jax.numpy as jnp
 from jax import lax
+from jax.experimental import pallas as pl
+from jax.experimental.pallas import tpu as pltpu
 from jax.sharding import PartitionSpec as P
 
 HEAD_SIZE = 128
@@ -96,8 +100,279 @@
     return lax.all_to_all(output_rows, "uly", split_axis=0, concat_axis=1, tiled=True)
 
 
+MESH = pl.DeviceIdType.MESH
+LOG2_E = 1.4426950408889634
+
+
+def attention_kernel(
+    pairs,
+    groups,
+    q_ref,
+    k_ref,
+    v_ref,
+    out_ref,
+    kv,
+    q_here,
+    o_here,
+    own_sem,
+    pair_send,
+    slot_sem,
+    send_sem,
+    q_sem,
+    o_sem,
+):
+    ctx = lax.axis_index("ctx")
+    half = lax.axis_index("uly")
+    other = 1 - half
+    pair, core = ctx // 2, lax.rem(ctx, 2)
+    odd = lax.rem(pair, 2)
+    chunks = kv.shape[0]
+    rows = q_ref.shape[0]
+    q_cols = q_ref.shape[1] // 2
+    wide = q_cols // chunks
+
+    mate = (2 * pair + 1 - core, half)
+    across = (ctx, other)
+    ahead1, ahead2 = (ctx + 2, half), (ctx + 4, half)
+    behind1, behind2 = (ctx - 2, half), (ctx - 4, half)
+    has_a1, has_a2 = pair + 1 < pairs, pair + 2 < pairs
+    has_b1, has_b2 = pair >= 1, pair >= 2
+    even = odd == 0
+    always = pair >= 0
+
+    barrier = pltpu.get_barrier_semaphore()
+    count = jnp.int32(0)
+    for device, exists in (
+        (mate, always),
+        (across, always),
+        (ahead1, has_a1),
+        (ahead2, has_a2),
+        (behind1, has_b1),
+        (behind2, has_b2),
+    ):
+        count += exists.astype(jnp.int32)
+
+        @pl.when(exists)
+        def _():
+            pl.semaphore_signal(barrier, inc=1, device_id=device, device_id_type=MESH)
+
+    def column(ref, head):
+        return ref.at[:, pl.ds(pl.multiple_of(head * HEAD_SIZE, HEAD_SIZE), HEAD_SIZE)]
+
+    def q_part(ref, index):
+        return ref.at[:, pl.ds(pl.multiple_of(index * q_cols, q_cols), q_cols)]
+
+    own = []
+    for chunk in range(chunks):
+        for which, ref in enumerate((k_ref, v_ref)):
+            copy = pltpu.make_async_copy(
+                column(ref, core * chunks + chunk),
+                kv.at[chunk, which, 1 - core, half],
+                own_sem.at[chunk, 1 - core, which],
+            )
+            copy.start()
+    q_own = pltpu.make_async_copy(q_part(q_ref, core), q_here.at[core], q_sem.at[0])
+    q_own.start()
+
+    @pl.when(pair < 2)
+    def _():
+        for d in (2, 3, 4):
+
+            @pl.when(2 * pair + 1 - d < 0)
+            def _():
+                kv[:, :, d] = jnp.zeros_like(kv[:, :, d])
+
+    pl.semaphore_wait(barrier, count)
+
+    pending = []
+
+    def send(src, dst, sent, landed, device, exists):
+        copy = pltpu.make_async_remote_copy(
+            src_ref=src, dst_ref=dst, send_sem=sent, recv_sem=landed, device_id=device, device_id_type=MESH
+        )
+
+        @pl.when(exists)
+        def _():
+            copy.start()
+
+        pending.append((copy, exists))
+
+    for chunk in range(chunks):
+        for which, ref in enumerate((k_ref, v_ref)):
+            send(
+                column(ref, (1 - core) * chunks + chunk),
+                kv.at[chunk, which, 1 - core, half],
+                pair_send.at[chunk, which],
+                own_sem.at[chunk, 1 - core, which],
+                mate,
+                always,
+            )
+    def await_own(chunk, d):
+        for which in range(2):
+            ref = kv.at[chunk, which, d, half]
+            pltpu.make_async_copy(ref, ref, own_sem.at[chunk, d, which]).wait()
+
+    def await_slot(chunk, d, side, exists=None):
+        ref = kv.at[chunk, :, d, side]
+        copy = pltpu.make_async_copy(ref, ref, slot_sem.at[chunk, d, side])
+        if exists is None:
+            copy.wait()
+        else:
+
+            @pl.when(exists)
+            def _():
+                copy.wait()
+
+    def pass_on(chunk, src_d, dst_d, side, route, device, exists):
+        send(
+            kv.at[chunk, :, src_d, side],
+            kv.at[chunk, :, dst_d, side],
+            send_sem.at[chunk, route],
+            slot_sem.at[chunk, dst_d, side],
+            device,
+            exists,
+        )
+
+    def origin(chunk):
+        await_own(chunk, 0)
+        pass_on(chunk, 0, 0, half, 0, across, always)
+        pass_on(chunk, 0, 4, half, 1, ahead2, has_a2)
+        pass_on(chunk, 0, 2, half, 2, ahead1, has_a1 & even)
+        await_own(chunk, 1)
+        pass_on(chunk, 1, 3, half, 3, ahead1, has_a1)
+        pass_on(chunk, 1, 1, half, 4, across, always)
+
+    def relay(chunk):
+        await_slot(chunk, 0, other)
+        pass_on(chunk, 0, 4, other, 5, ahead2, has_a2)
+        pass_on(chunk, 0, 2, other, 6, ahead1, has_a1 & even)
+        await_slot(chunk, 3, half, has_b1)
+        pass_on(chunk, 3, 3, half, 7, across, has_b1)
+        from_far = has_b2 & (odd == 1)
+        await_slot(chunk, 4, half, from_far)
+        pass_on(chunk, 4, 2, half, 8, behind1, from_far)
+        await_slot(chunk, 4, other, from_far)
+        pass_on(chunk, 4, 2, other, 9, behind1, from_far)
+
+    def gather(chunk):
+        await_slot(chunk, 1, other)
+        await_slot(chunk, 4, half, has_b2 & even)
+        await_slot(chunk, 4, other, has_b2 & even)
+        await_slot(chunk, 3, other, has_b1)
+        await_slot(chunk, 2, half, has_b1)
+        await_slot(chunk, 2, other, has_b1)
+
+    factor = HEAD_SIZE ** (-0.5) * LOG2_E
+    keys = 8 * rows
+
+    def attend(chunk):
+        def body(index, _):
+            side, head = index // groups, lax.rem(index, groups)
+            first = 1 - side
+            cols = pl.ds(pl.multiple_of(chunk * wide + head * HEAD_SIZE, HEAD_SIZE), HEAD_SIZE)
+            query = q_here[side, :, cols]
+            key = kv[chunk, 0, pl.ds(first, 4)].reshape(keys, HEAD_SIZE)
+            value = kv[chunk, 1, pl.ds(first, 4)].reshape(keys, HEAD_SIZE)
+            scores = lax.dot_general(
+                query, key, (((1,), (1,)), ((), ())), preferred_element_type=jnp.float32
+            )
+            row = lax.broadcasted_iota(jnp.int32, (rows, keys), 0)
+            col = lax.broadcasted_iota(jnp.int32, (rows, keys), 1)
+            limit = jnp.minimum(2 * pair + side + 1, WINDOW_BLOCKS + 1) * (2 * rows)
+            visible = (col < limit) & ((col <= row + half * rows) | (col >= 2 * rows))
+            scores = jnp.where(visible, scores, -jnp.inf)
+            top = jnp.max(scores, axis=1, keepdims=True)
+            weights = jnp.exp2((scores - top) * factor).astype(jnp.bfloat16)
+            extended = jnp.concatenate([value, jnp.ones_like(value)], axis=1)
+            mixed = jnp.dot(weights, extended, preferred_element_type=jnp.float32)
+            o_here[side, :, cols] = (mixed[:, :HEAD_SIZE] / mixed[:, HEAD_SIZE:]).astype(jnp.bfloat16)
+            return 0
+
+        lax.fori_loop(0, 2 * groups, body, 0)
+
+    outs = []
+
+    def give(chunk):
+        here = pl.ds(chunk * wide, wide)
+        there = pl.ds(pl.multiple_of(core * q_cols + chunk * wide, wide), wide)
+        copy = pltpu.make_async_copy(o_here.at[core, :, here], out_ref.at[:, there], o_sem.at[0, chunk])
+        copy.start()
+        outs.append(copy)
+        send(
+            o_here.at[1 - core, :, here],
+            out_ref.at[:, there],
+            o_sem.at[1, chunk],
+            o_sem.at[2, chunk],
+            mate,
+            always,
+        )
+
+    for chunk in range(chunks):
+        origin(chunk)
+        if chunk == 0:
+            send(q_part(q_ref, 1 - core), q_here.at[core], q_sem.at[1], q_sem.at[2], mate, always)
+    for chunk in range(chunks):
+        relay(chunk)
+        if chunk == 1:
+            q_own.wait()
+            pltpu.make_async_copy(q_here.at[1 - core], q_here.at[1 - core], q_sem.at[2]).wait()
+        if chunk > 0:
+            gather(chunk - 1)
+            attend(chunk - 1)
+            give(chunk - 1)
+    gather(chunks - 1)
+    attend(chunks - 1)
+    give(chunks - 1)
+
+    for copy, exists in pending:
+
+        @pl.when(exists)
+        def _():
+            copy.wait_send()
+
+    for chunk in range(chunks):
+        outs[chunk].wait()
+        there = pl.ds(pl.multiple_of((1 - core) * q_cols + chunk * wide, wide), wide)
+        ref = out_ref.at[:, there]
+        pltpu.make_async_copy(ref, ref, o_sem.at[2, chunk]).wait()
+
+
+def on_device_pairs(blocks, queries, keys, values):
+    rows = queries.shape[0]
+    kv_heads = keys.shape[1] // HEAD_SIZE
+    groups = queries.shape[1] // keys.shape[1]
+    chunks = kv_heads // 2
+    dma = pltpu.SemaphoreType.DMA
+    flops = 4 * rows * queries.shape[1] * 8 * rows
+    return pl.pallas_call(
+        functools.partial(attention_kernel, blocks // 2, groups),
+        out_shape=jax.ShapeDtypeStruct(queries.shape, queries.dtype),
+        in_specs=[pl.BlockSpec(memory_space=pl.ANY)] * 3,
+        out_specs=pl.BlockSpec(memory_space=pl.ANY),
+        scratch_shapes=[
+            pltpu.VMEM((chunks, 2, 5, 2, rows, HEAD_SIZE), jnp.bfloat16),
+            pltpu.VMEM((2, rows, queries.shape[1] // 2), jnp.bfloat16),
+            pltpu.VMEM((2, rows, queries.shape[1] // 2), jnp.bfloat16),
+            dma((chunks, 2, 2)),
+            dma((chunks, 2)),
+            dma((chunks, 5, 2)),
+            dma((chunks, 10)),
+            dma((3,)),
+            dma((3, chunks)),
+        ],
+        compiler_params=pltpu.CompilerParams(
+            collective_id=0, has_side_effects=True, vmem_limit_bytes=40 * 2**20
+        ),
+        cost_estimate=pl.CostEstimate(flops=flops, bytes_accessed=6 * queries.size, transcendentals=flops // 512),
+    )(queries, keys, values)
+
+
 def solution(mesh):
     placed = (P(("ctx", "uly"), None), P(("ctx", "uly"), None), P(("ctx", "uly"), None))
+    blocks, halves = mesh.shape["ctx"], mesh.shape["uly"]
+    body = on_device
+    if halves == 2 and blocks % 4 == 0:
+        body = functools.partial(on_device_pairs, blocks)
     return jax.shard_map(
-        on_device, mesh=mesh, in_specs=placed, out_specs=P(("ctx", "uly"), None), check_vma=False
-    )
+        body, mesh=mesh, in_specs=placed, out_specs=P(("ctx", "uly"), None), check_vma=False
+    )

time: 413 us -> 49.2 us (0.12)
  the two profiles are of different devices: /device:TPU:0 before, /device:TPU:21 now
where the time goes in v1:
time: 49.2 us; the launch traced here: 49 us
  Pallas kernels  44.9 us (91%)
  local copies, waits for them, and re-layouts  4.1 us (8%)
    pallas_call x1, Pallas kernels, on_device_pairs(): pl.pallas_call(functools.partial(attention_kernel, blocks // 2, groups),...  44.9 us
    unnamed x7, local copies, waits for them, and re-layouts  4.1 us

profile of v1, /device:TPU:21, one launch (start us, length us, event | category | flops | bytes accessed | tf_op | source)
XLA Modules:
  0.0 49.0 jit_solution(11225237344444089374)
XLA Ops:
  0.0 0.0 copy-start
  0.0 1.2 %copy-done = bf16[128,4096]{1,0:T(8,128)(2,1)S(1)} copy-done((bf16[128,4096]{1,0:T(8,128)(2,1)S(1)}, bf16[128,4096]{1,0:T(8,128)(2,1)}, u32[]{:S(2)}) %copy-start) | copy-done | bytes 1048600
  1.2 0.0 copy-start.1
  1.2 0.9 %copy-done.1 = bf16[128,1024]{1,0:T(8,128)(2,1)S(1)} copy-done((bf16[128,1024]{1,0:T(8,128)(2,1)S(1)}, bf16[128,1024]{1,0:T(8,128)(2,1)}, u32[]{:S(2)}) %copy-start.1) | copy-done | bytes 262168
  2.2 0.0 copy-start.2
  2.2 0.9 %copy-done.2 = bf16[128,1024]{1,0:T(8,128)(2,1)S(1)} copy-done((bf16[128,1024]{1,0:T(8,128)(2,1)S(1)}, bf16[128,1024]{1,0:T(8,128)(2,1)}, u32[]{:S(2)}) %copy-start.2) | copy-done | bytes 262168
  3.1 44.9 %shard_map.37 = bf16[128,4096]{1,0:T(8,128)(2,1)S(1)} custom-call(bf16[128,4096]{1,0:T(8,128)(2,1)S(1)} %copy-done, bf16[128,1024]{1,0:T(8,128)(2,1)S(1)} %copy-done.1, bf16[128,1024]{1,0:T(8,128)(2,1)S(1)} %copy-done.2), custom_call_target="tpu_custom_call" | custom-call | flops 2147483648 | bytes 3145728 | tf_op jit(solution)/shard_map/pallas_call | solution.py:347
  48.0 1.0 %copy.5 = bf16[128,4096]{1,0:T(8,128)(2,1)} copy(bf16[128,4096]{1,0:T(8,128)(2,1)S(1)} %shard_map.37) | data formatting | bytes 2097152
Async XLA Ops:
  0.0 1.2 %copy-start = (bf16[128,4096]{1,0:T(8,128)(2,1)S(1)}, bf16[128,4096]{1,0:T(8,128)(2,1)}, u32[]{:S(2)}) copy-start(bf16[128,4096]{1,0:T(8,128)(2,1)} %q_ref.1) | copy-start | bytes 3145732
  1.2 0.9 %copy-start.1 = (bf16[128,1024]{1,0:T(8,128)(2,1)S(1)}, bf16[128,1024]{1,0:T(8,128)(2,1)}, u32[]{:S(2)}) copy-start(bf16[128,1024]{1,0:T(8,128)(2,1)} %k_ref.1) | copy-start | bytes 786436
  2.2 0.9 %copy-start.2 = (bf16[128,1024]{1,0:T(8,128)(2,1)S(1)}, bf16[128,1024]{1,0:T(8,128)(2,1)}, u32[]{:S(2)}) copy-start(bf16[128,1024]{1,0:T(8,128)(2,1)} %v_ref.1) | copy-start | bytes 786436

commit v2 on v1

--- a/solution.py
+++ b/solution.py
@@ -114,6 +114,8 @@
     kv,
     q_here,
     o_here,
+    bias,
+    counted,
     own_sem,
     pair_send,
     slot_sem,
@@ -180,7 +182,7 @@
 
             @pl.when(2 * pair + 1 - d < 0)
             def _():
-                kv[:, :, d] = jnp.zeros_like(kv[:, :, d])
+                kv[:, 1, d] = jnp.zeros_like(kv[:, 1, d])
 
     pl.semaphore_wait(barrier, count)
 
@@ -264,31 +266,54 @@
 
     factor = HEAD_SIZE ** (-0.5) * LOG2_E
     keys = 8 * rows
+    row = lax.broadcasted_iota(jnp.int32, bias.shape, 0)
+    col = lax.broadcasted_iota(jnp.int32, bias.shape, 1)
+    bias[...] = jnp.where(col <= row + half * rows, 0.0, -1e30)
+    counted[...] = jnp.ones_like(counted)
+
+    @pl.when(pair < 2)
+    def _():
+        for d in (2, 3, 4):
+
+            @pl.when(2 * pair + 1 - d < 0)
+            def _():
+                counted[d] = jnp.zeros_like(counted[d])
 
     def attend(chunk):
-        def body(index, _):
-            side, head = index // groups, lax.rem(index, groups)
+        @pl.when(pair < 2)
+        def _():
+            seen = jnp.broadcast_to(kv[chunk, 0, 1, 0][:1], (rows, HEAD_SIZE))
+            for d in (2, 3, 4):
+
+                @pl.when(2 * pair + 1 - d < 0)
+                def _():
+                    kv[chunk, 0, d, 0] = seen
+                    kv[chunk, 0, d, 1] = seen
+
+        for side in range(2):
             first = 1 - side
-            cols = pl.ds(pl.multiple_of(chunk * wide + head * HEAD_SIZE, HEAD_SIZE), HEAD_SIZE)
-            query = q_here[side, :, cols]
-            key = kv[chunk, 0, pl.ds(first, 4)].reshape(keys, HEAD_SIZE)
-            value = kv[chunk, 1, pl.ds(first, 4)].reshape(keys, HEAD_SIZE)
+            heads = [pl.ds(chunk * wide + head * HEAD_SIZE, HEAD_SIZE) for head in range(groups)]
+            query = jnp.concatenate([q_here[side, :, cols] for cols in heads], axis=0)
+            key = kv[chunk, 0, first : first + 4].reshape(keys, HEAD_SIZE)
+            value = kv[chunk, 1, first : first + 4].reshape(keys, HEAD_SIZE)
+            ones = counted[first : first + 4].reshape(keys, HEAD_SIZE)
             scores = lax.dot_general(
                 query, key, (((1,), (1,)), ((), ())), preferred_element_type=jnp.float32
             )
-            row = lax.broadcasted_iota(jnp.int32, (rows, keys), 0)
-            col = lax.broadcasted_iota(jnp.int32, (rows, keys), 1)
-            limit = jnp.minimum(2 * pair + side + 1, WINDOW_BLOCKS + 1) * (2 * rows)
-            visible = (col < limit) & ((col <= row + half * rows) | (col >= 2 * rows))
-            scores = jnp.where(visible, scores, -jnp.inf)
-            top = jnp.max(scores, axis=1, keepdims=True)
-            weights = jnp.exp2((scores - top) * factor).astype(jnp.bfloat16)
-            extended = jnp.concatenate([value, jnp.ones_like(value)], axis=1)
-            mixed = jnp.dot(weights, extended, preferred_element_type=jnp.float32)
-            o_here[side, :, cols] = (mixed[:, :HEAD_SIZE] / mixed[:, HEAD_SIZE:]).astype(jnp.bfloat16)
-            return 0
-
-        lax.fori_loop(0, 2 * groups, body, 0)
+            parts = []
+            for head in range(groups):
+                part = scores[head * rows : (head + 1) * rows]
+                part = jnp.concatenate([part[:, : 2 * rows] + bias[...], part[:, 2 * rows :]], axis=1)
+                top = jnp.max(part, axis=1, keepdims=True)
+                parts.append(jnp.exp2((part - top) * factor).astype(jnp.bfloat16))
+            mixed = jnp.dot(
+                jnp.concatenate(parts, axis=0),
+                jnp.concatenate([value, ones], axis=1),
+                preferred_element_type=jnp.float32,
+            )
+            result = (mixed[:, :HEAD_SIZE] / mixed[:, HEAD_SIZE:]).astype(jnp.bfloat16)
+            for head, cols in enumerate(heads):
+                o_here[side, :, cols] = result[head * rows : (head + 1) * rows]
 
     outs = []
 
@@ -347,12 +372,14 @@
     return pl.pallas_call(
         functools.partial(attention_kernel, blocks // 2, groups),
         out_shape=jax.ShapeDtypeStruct(queries.shape, queries.dtype),
-        in_specs=[pl.BlockSpec(memory_space=pl.ANY)] * 3,
-        out_specs=pl.BlockSpec(memory_space=pl.ANY),
+        in_specs=[pl.BlockSpec(memory_space=pltpu.HBM)] * 3,
+        out_specs=pl.BlockSpec(memory_space=pltpu.HBM),
         scratch_shapes=[
             pltpu.VMEM((chunks, 2, 5, 2, rows, HEAD_SIZE), jnp.bfloat16),
             pltpu.VMEM((2, rows, queries.shape[1] // 2), jnp.bfloat16),
             pltpu.VMEM((2, rows, queries.shape[1] // 2), jnp.bfloat16),
+            pltpu.VMEM((rows, 2 * rows), jnp.float32),
+            pltpu.VMEM((5, 2, rows, HEAD_SIZE), jnp.bfloat16),
             dma((chunks, 2, 2)),
             dma((chunks, 2)),
             dma((chunks, 5, 2)),
@@ -361,7 +388,7 @@
             dma((3, chunks)),
         ],
         compiler_params=pltpu.CompilerParams(
-            collective_id=0, has_side_effects=True, vmem_limit_bytes=40 * 2**20
+            collective_id=0, has_side_effects=True, vmem_limit_bytes=60 * 2**20
         ),
         cost_estimate=pl.CostEstimate(flops=flops, bytes_accessed=6 * queries.size, transcendentals=flops // 512),
     )(queries, keys, values)

time: 49.2 us -> 37.7 us (0.77)
  the two profiles are of different devices: /device:TPU:21 before, /device:TPU:17 now
where the time goes in v2:
time: 37.7 us; the launch traced here: 37.6 us
  Pallas kernels  35.3 us (94%)
  local copies, waits for them, and re-layouts  2.29 us (6%)
    pallas_call x1, Pallas kernels, on_device_pairs(): pl.pallas_call(functools.partial(attention_kernel, blocks // 2, groups),...  35.3 us
    unnamed x1, local copies, waits for them, and re-layouts  2.29 us

profile of v2, /device:TPU:17, one launch (start us, length us, event | category | flops | bytes accessed | tf_op | source)
XLA Modules:
  0.0 37.6 jit_solution(6227305065539845356)
XLA Ops:
  0.0 35.3 %shard_map.37 = bf16[128,4096]{1,0:T(8,128)(2,1)} custom-call(bf16[128,4096]{1,0:T(8,128)(2,1)} %q_ref.1, bf16[128,1024]{1,0:T(8,128)(2,1)} %k_ref.1, bf16[128,1024]{1,0:T(8,128)(2,1)} %v_ref.1), custom_call_target="tpu_custom_call" | custom-call | flops 2147483648 | bytes 3145728 | tf_op jit(solution)/shard_map/pallas_call | solution.py:372
  35.3 2.3 %copy.5 = bf16[128,4096]{1,0:T(8,128)(2,1)} copy(bf16[128,4096]{1,0:T(8,128)(2,1)} %shard_map.37) | data formatting | bytes 2097152

commit v3 on v2

--- a/solution.py
+++ b/solution.py
@@ -235,24 +235,33 @@
             exists,
         )
 
+    from_far = has_b2 & (odd == 1)
+
     def origin(chunk):
         await_own(chunk, 0)
         pass_on(chunk, 0, 0, half, 0, across, always)
         pass_on(chunk, 0, 4, half, 1, ahead2, has_a2)
-        pass_on(chunk, 0, 2, half, 2, ahead1, has_a1 & even)
         await_own(chunk, 1)
         pass_on(chunk, 1, 3, half, 3, ahead1, has_a1)
+        pass_on(chunk, 0, 2, half, 2, ahead1, has_a1 & even)
+
+    def cross_last(chunk):
         pass_on(chunk, 1, 1, half, 4, across, always)
 
-    def relay(chunk):
+    def relay_first(chunk):
         await_slot(chunk, 0, other)
         pass_on(chunk, 0, 4, other, 5, ahead2, has_a2)
         pass_on(chunk, 0, 2, other, 6, ahead1, has_a1 & even)
+
+    def relay_cross(chunk):
         await_slot(chunk, 3, half, has_b1)
         pass_on(chunk, 3, 3, half, 7, across, has_b1)
-        from_far = has_b2 & (odd == 1)
+
+    def relay_own(chunk):
         await_slot(chunk, 4, half, from_far)
         pass_on(chunk, 4, 2, half, 8, behind1, from_far)
+
+    def relay_other(chunk):
         await_slot(chunk, 4, other, from_far)
         pass_on(chunk, 4, 2, other, 9, behind1, from_far)
 
@@ -332,23 +341,35 @@
             always,
         )
 
-    for chunk in range(chunks):
-        origin(chunk)
-        if chunk == 0:
-            send(q_part(q_ref, 1 - core), q_here.at[core], q_sem.at[1], q_sem.at[2], mate, always)
-    for chunk in range(chunks):
-        relay(chunk)
-        if chunk == 1:
-            q_own.wait()
-            pltpu.make_async_copy(q_here.at[1 - core], q_here.at[1 - core], q_sem.at[2]).wait()
-        if chunk > 0:
-            gather(chunk - 1)
-            attend(chunk - 1)
-            give(chunk - 1)
-    gather(chunks - 1)
-    attend(chunks - 1)
-    give(chunks - 1)
-
+    def ask(_):
+        send(q_part(q_ref, 1 - core), q_here.at[core], q_sem.at[1], q_sem.at[2], mate, always)
+
+    def await_queries(_):
+        q_own.wait()
+        pltpu.make_async_copy(q_here.at[1 - core], q_here.at[1 - core], q_sem.at[2]).wait()
+
+    def finish(chunk):
+        gather(chunk)
+        attend(chunk)
+        give(chunk)
+
+    for chunk in range(chunks + 2):
+        if chunk < chunks:
+            origin(chunk)
+            if chunk == 0:
+                ask(chunk)
+        if 0 < chunk <= chunks:
+            relay_first(chunk - 1)
+            relay_cross(chunk - 1)
+            relay_own(chunk - 1)
+            cross_last(chunk - 1)
+        if 1 < chunk:
+            relay_other(chunk - 2)
+            if chunk == 2:
+                await_queries(chunk)
+            if chunk > 2:
+                finish(chunk - 3)
+    finish(chunks - 1)
     for copy, exists in pending:
 
         @pl.when(exists)
@@ -369,11 +390,12 @@
     chunks = kv_heads // 2
     dma = pltpu.SemaphoreType.DMA
     flops = 4 * rows * queries.shape[1] * 8 * rows
+    queries, keys, values = (pltpu.with_memory_space_constraint(a, pltpu.HBM) for a in (queries, keys, values))
     return pl.pallas_call(
         functools.partial(attention_kernel, blocks // 2, groups),
         out_shape=jax.ShapeDtypeStruct(queries.shape, queries.dtype),
         in_specs=[pl.BlockSpec(memory_space=pltpu.HBM)] * 3,
-        out_specs=pl.BlockSpec(memory_space=pltpu.HBM),
+        out_specs=pl.BlockSpec(memory_space=pl.ANY),
         scratch_shapes=[
             pltpu.VMEM((chunks, 2, 5, 2, rows, HEAD_SIZE), jnp.bfloat16),
             pltpu.VMEM((2, rows, queries.shape[1] // 2), jnp.bfloat16),
@@ -388,7 +410,7 @@
             dma((3, chunks)),
         ],
         compiler_params=pltpu.CompilerParams(
-            collective_id=0, has_side_effects=True, vmem_limit_bytes=60 * 2**20
+            collective_id=0, has_side_effects=True, vmem_limit_bytes=32 * 2**20
         ),
         cost_estimate=pl.CostEstimate(flops=flops, bytes_accessed=6 * queries.size, transcendentals=flops // 512),
     )(queries, keys, values)

time: 37.7 us -> 30.9 us (0.82)
  Pallas kernels: 35.3 us -> 29.7 us
  local copies, waits for them, and re-layouts: 2.29 us -> 0.97 us
    pallas_call x1, Pallas kernels: 35.3 us -> 29.7 us  [on_device_pairs(): pl.pallas_call(functools.partial(attention_kernel, blocks // 2, groups),...]
    unnamed x1, local copies, waits for them, and re-layouts: 2.29 us -> 0.97 us
where the time goes in v3:
time: 30.9 us; the launch traced here: 30.7 us
  Pallas kernels  29.7 us (96%)
  local copies, waits for them, and re-layouts  0.97 us (3%)
    pallas_call x1, Pallas kernels, on_device_pairs(): pl.pallas_call(functools.partial(attention_kernel, blocks // 2, groups),...  29.7 us
    unnamed x1, local copies, waits for them, and re-layouts  0.97 us

profile of v3, /device:TPU:17, one launch (start us, length us, event | category | flops | bytes accessed | tf_op | source)
XLA Modules:
  0.0 30.7 jit_solution(4700722458242201546)
XLA Ops:
  0.0 29.7 %shard_map.37 = bf16[128,4096]{1,0:T(8,128)(2,1)S(1)} custom-call(bf16[128,4096]{1,0:T(8,128)(2,1)} %q_ref.1, bf16[128,1024]{1,0:T(8,128)(2,1)} %k_ref.1, bf16[128,1024]{1,0:T(8,128)(2,1)} %v_ref.1), custom_call_target="tpu_custom_call" | custom-call | flops 2147483648 | bytes 3145728 | tf_op jit(solution)/shard_map/pallas_call | solution.py:394
  29.7 1.0 %copy.5 = bf16[128,4096]{1,0:T(8,128)(2,1)} copy(bf16[128,4096]{1,0:T(8,128)(2,1)S(1)} %shard_map.37) | data formatting | bytes 2097152

commit v4 on v3

--- a/solution.py
+++ b/solution.py
@@ -362,9 +362,9 @@
             relay_first(chunk - 1)
             relay_cross(chunk - 1)
             relay_own(chunk - 1)
-            cross_last(chunk - 1)
         if 1 < chunk:
             relay_other(chunk - 2)
+            cross_last(chunk - 2)
             if chunk == 2:
                 await_queries(chunk)
             if chunk > 2:

time: 30.9 us -> 30.9 us (level)
  no operation moved by 1% of the time
where the time goes in v4:
time: 30.9 us; the launch traced here: 30.7 us
  Pallas kernels  29.7 us (96%)
  local copies, waits for them, and re-layouts  0.97 us (3%)
    pallas_call x1, Pallas kernels, on_device_pairs(): pl.pallas_call(functools.partial(attention_kernel, blocks // 2, groups),...  29.7 us
    unnamed x1, local copies, waits for them, and re-layouts  0.97 us

profile of v4, /device:TPU:17, one launch (start us, length us, event | category | flops | bytes accessed | tf_op | source)
XLA Modules:
  0.0 30.7 jit_solution(12879590501510038379)
XLA Ops:
  0.0 29.7 %shard_map.37 = bf16[128,4096]{1,0:T(8,128)(2,1)S(1)} custom-call(bf16[128,4096]{1,0:T(8,128)(2,1)} %q_ref.1, bf16[128,1024]{1,0:T(8,128)(2,1)} %k_ref.1, bf16[128,1024]{1,0:T(8,128)(2,1)} %v_ref.1), custom_call_target="tpu_custom_call" | custom-call | flops 2147483648 | bytes 3145728 | tf_op jit(solution)/shard_map/pallas_call | solution.py:394
  29.7 1.0 %copy.5 = bf16[128,4096]{1,0:T(8,128)(2,1)} copy(bf16[128,4096]{1,0:T(8,128)(2,1)S(1)} %shard_map.37) | data formatting | bytes 2097152
